TPU v7x, 512 devices: a whole 4x4x16 slice. The times are simulated.
512 devices in a mesh: dp: 32 (over z, core), fsdp: 16 (over x, y).
Axes of the slice: x: 4, y: 4, z: 16, core: 2. Of those that a mesh axis runs over, the one named last changes fastest.
Arguments:
- token_ids: int32 [65536], P(('dp', 'fsdp')), may hold values from 0 to 50431, as said below
- activations: bfloat16 [65536, 3072], P(('dp', 'fsdp'))
- grad_out: bfloat16 [65536, 3072], P(('dp', 'fsdp')), may hold values from -0.13183594 to 0.13183594
- error_buffer: bfloat16 [32, 3072, 3072], P('dp', 'fsdp'), may hold values from -6 to 6
- init_q: float32 [3072, 8], replicated, may hold values from -6 to 6
Outputs:
- p_factor: float32 [3072, 8], P('fsdp')
- q_factor: float32 [3072, 8], replicated
- error_next: bfloat16 [32, 3072, 3072], P('dp', 'fsdp')
Inputs may be any that keep to these rules, and one draw needn't show every extreme that they name: `token_ids`: id 1 is padding; on the rows of each device it forms a tail (possibly empty), and each device's first row holds id 0.
All inputs are finite; a program needn't handle non-finite values.
Results may differ from a plain program's by a relative error of at most 0.0006.
Values may be sent and summed in bfloat16 or wider, within the bound.
No kernel may reach another device: no remote copies, remote signals or barrier semaphores. Data moves between devices by JAX's collectives and lax.ppermute only.
A program may use at most 64 MiB of HBM per device.

v0:
```python
import jax
import jax.numpy as jnp
from jax import lax
from jax.sharding import PartitionSpec as P


def orthonormal_columns(p_rows):
    highest = lax.Precision.HIGHEST
    finished = []
    for index_col in range(p_rows.shape[1]):
        column = p_rows[:, index_col]
        if finished:
            stacked = jnp.stack(finished, axis=1)
            inner_vals = lax.psum(jnp.dot(column, stacked, precision=highest), "fsdp")
            column = column - jnp.dot(stacked, inner_vals, precision=highest)
        norm_square = lax.psum(jnp.sum(column * column), "fsdp")
        finished.append(column / jnp.sqrt(norm_square))
    return jnp.stack(finished, axis=1)


def on_device(token_ids, activations, grad_out, error_buffer, init_q):
    highest = lax.Precision.HIGHEST
    replicas = lax.axis_size("dp")
    valid_rows = (token_ids != 1).astype(grad_out.dtype)
    masked_grad = grad_out * valid_rows[:, None]
    x_cols = lax.all_to_all(activations, "fsdp", split_axis=1, concat_axis=0, tiled=True)
    error_rows = error_buffer[0]
    grad_rows = lax.dot_general(
        x_cols,
        lax.all_gather(masked_grad, "fsdp", axis=0, tiled=True),
        (((0,), (0,)), ((), ())),
        preferred_element_type=jnp.float32,
    )
    merged = grad_rows + error_rows.astype(jnp.float32)
    p_local = jnp.dot(merged, init_q, precision=highest)
    p_mean = lax.psum(p_local, "dp") / replicas
    ortho_basis = orthonormal_columns(p_mean)
    q_local = jnp.einsum(
        "rd,rk->dk", merged, ortho_basis, precision=highest, preferred_element_type=jnp.float32
    )
    q_factor = lax.psum(q_local, ("dp", "fsdp")) / replicas
    error_next = (merged - jnp.dot(ortho_basis, q_factor.T, precision=highest)).astype(jnp.bfloat16)
    return (ortho_basis, q_factor, error_next[None])


def solution(mesh):
    return jax.shard_map(
        on_device,
        mesh=mesh,
        in_specs=(
            P(("dp", "fsdp")),
            P(("dp", "fsdp"), None),
            P(("dp", "fsdp"), None),
            P("dp", "fsdp", None),
            P(),
        ),
        out_specs=(P("fsdp", None), P(), P("dp", "fsdp", None)),
        check_vma=False,
    )
```

profile of v0, /device:TPU:1, one launch (start us, length us, event | category | flops | bytes accessed | tf_op | source)
XLA Modules:
  0.0 1197.7 jit_solution(5980001329945168853)
XLA Ops:
  8.0 2.1 broadcast_multiply_fusion
  10.6 19.1 %all_to_all.19 = bf16[128,16,192]{0,2,1:T(8,128)(2,1)S(1)} all-to-all(bf16[128,16,192]{0,2,1:T(8,128)(2,1)S(1)} %bitcast.83), channel_id=1, replica_groups=mesh['dp'=32,'fsdp'=16] {'fsdp'}, dimensions={1} | all-to-all | bytes 1572864 | tf_op jit(solution)/shard_map/all_to_all | solution.py:26
  29.7 92.6 %all-gather.2.cloned.1.call-done = bf16[2048,3072]{1,0:T(8,128)(2,1)} async-done(((bf16[128,3072]{1,0:T(8,128)(2,1)}), bf16[2048,3072]{1,0:T(8,128)(2,1)}) %all-gather.2.cloned.1.call-update) | async-done | bytes 12582928 | tf_op jit(solution)/shard_map/all_gather | solution.py:30
  122.3 7.6 fusion
  130.0 1.9 fusion.29
  131.9 48.0 %psum.119 = f32[192,8]{0,1:T(8,128)S(1)} all-reduce(f32[192,8]{0,1:T(8,128)S(1)} %fusion.29), channel_id=1, replica_groups=mesh['dp'=32,'fsdp'=16] {'dp'}, use_global_device_ids=true, to_apply=%region_0.0 | all-reduce | flops 1536 | bytes 12288 | tf_op jit(solution)/shard_map/psum | solution.py:36
  180.5 31.8 %psum.120 = f32[]{:T(128)} all-reduce(f32[]{:T(128)} %multiply_reduce_fusion.8), channel_id=1, replica_groups=mesh['dp'=32,'fsdp'=16] {'fsdp'}, use_global_device_ids=true, to_apply=%region_2.0 | all-reduce | flops 1 | bytes 8 | tf_op jit(solution)/shard_map/psum | solution.py:16
  213.6 29.1 %psum.121 = f32[]{:T(128)} all-reduce(f32[]{:T(128)} %multiply_reduce_fusion), channel_id=1, replica_groups=mesh['dp'=32,'fsdp'=16] {'fsdp'}, use_global_device_ids=true, to_apply=%region_3.0 | all-reduce | flops 1 | bytes 8 | tf_op jit(solution)/shard_map/psum | solution.py:14
  244.0 30.6 %psum.122 = f32[]{:T(128)} all-reduce(f32[]{:T(128)} %multiply_reduce_fusion.7), channel_id=1, replica_groups=mesh['dp'=32,'fsdp'=16] {'fsdp'}, use_global_device_ids=true, to_apply=%region_5.0 | all-reduce | flops 1 | bytes 8 | tf_op jit(solution)/shard_map/psum | solution.py:16
  276.1 29.1 %psum.123 = f32[2]{0:T(128)S(1)} all-reduce(f32[2]{0:T(128)S(1)} %convolution_bitcast_fusion.6), channel_id=1, replica_groups=mesh['dp'=32,'fsdp'=16] {'fsdp'}, use_global_device_ids=true, to_apply=%region_6.0 | all-reduce | flops 2 | bytes 16 | tf_op jit(solution)/shard_map/psum | solution.py:14
  305.9 30.0 %psum.124 = f32[]{:T(128)} all-reduce(f32[]{:T(128)} %get-tuple-element.13), channel_id=1, replica_groups=mesh['dp'=32,'fsdp'=16] {'fsdp'}, use_global_device_ids=true, to_apply=%region_8.0 | all-reduce | flops 1 | bytes 8 | tf_op jit(solution)/shard_map/psum | solution.py:16
  336.7 29.1 %psum.125 = f32[3]{0:T(128)S(1)} all-reduce(f32[3]{0:T(128)S(1)} %convolution_bitcast_fusion.5), channel_id=1, replica_groups=mesh['dp'=32,'fsdp'=16] {'fsdp'}, use_global_device_ids=true, to_apply=%region_9.0 | all-reduce | flops 3 | bytes 24 | tf_op jit(solution)/shard_map/psum | solution.py:14
  366.5 30.0 %psum.126 = f32[]{:T(128)} all-reduce(f32[]{:T(128)} %get-tuple-element.11), channel_id=1, replica_groups=mesh['dp'=32,'fsdp'=16] {'fsdp'}, use_global_device_ids=true, to_apply=%region_11.0 | all-reduce | flops 1 | bytes 8 | tf_op jit(solution)/shard_map/psum | solution.py:16
  397.3 29.5 %psum.127 = f32[4]{0:T(128)S(1)} all-reduce(f32[4]{0:T(128)S(1)} %convolution_bitcast_fusion.4), channel_id=1, replica_groups=mesh['dp'=32,'fsdp'=16] {'fsdp'}, use_global_device_ids=true, to_apply=%region_12.0 | all-reduce | flops 4 | bytes 32 | tf_op jit(solution)/shard_map/psum | solution.py:14
  427.6 29.6 %psum.128 = f32[]{:T(128)} all-reduce(f32[]{:T(128)} %get-tuple-element.9), channel_id=1, replica_groups=mesh['dp'=32,'fsdp'=16] {'fsdp'}, use_global_device_ids=true, to_apply=%region_14.0 | all-reduce | flops 1 | bytes 8 | tf_op jit(solution)/shard_map/psum | solution.py:16
  458.0 29.8 %psum.129 = f32[5]{0:T(128)S(1)} all-reduce(f32[5]{0:T(128)S(1)} %convolution_bitcast_fusion.3), channel_id=1, replica_groups=mesh['dp'=32,'fsdp'=16] {'fsdp'}, use_global_device_ids=true, to_apply=%region_15.0 | all-reduce | flops 5 | bytes 40 | tf_op jit(solution)/shard_map/psum | solution.py:14
  488.5 29.3 %psum.130 = f32[]{:T(128)} all-reduce(f32[]{:T(128)} %get-tuple-element.7), channel_id=1, replica_groups=mesh['dp'=32,'fsdp'=16] {'fsdp'}, use_global_device_ids=true, to_apply=%region_17.0 | all-reduce | flops 1 | bytes 8 | tf_op jit(solution)/shard_map/psum | solution.py:16
  518.7 30.6 %psum.131 = f32[6]{0:T(128)S(1)} all-reduce(f32[6]{0:T(128)S(1)} %convolution_bitcast_fusion.2), channel_id=1, replica_groups=mesh['dp'=32,'fsdp'=16] {'fsdp'}, use_global_device_ids=true, to_apply=%region_18.0 | all-reduce | flops 6 | bytes 48 | tf_op jit(solution)/shard_map/psum | solution.py:14
  550.0 29.3 %psum.132 = f32[]{:T(128)} all-reduce(f32[]{:T(128)} %get-tuple-element.5), channel_id=1, replica_groups=mesh['dp'=32,'fsdp'=16] {'fsdp'}, use_global_device_ids=true, to_apply=%region_20.0 | all-reduce | flops 1 | bytes 8 | tf_op jit(solution)/shard_map/psum | solution.py:16
  580.2 30.5 %psum.133 = f32[7]{0:T(128)S(1)} all-reduce(f32[7]{0:T(128)S(1)} %convolution_bitcast_fusion.1), channel_id=1, replica_groups=mesh['dp'=32,'fsdp'=16] {'fsdp'}, use_global_device_ids=true, to_apply=%region_21.0 | all-reduce | flops 7 | bytes 56 | tf_op jit(solution)/shard_map/psum | solution.py:14
  611.5 29.1 %psum.134 = f32[]{:T(128)} all-reduce(f32[]{:T(128)} %get-tuple-element.3), channel_id=1, replica_groups=mesh['dp'=32,'fsdp'=16] {'fsdp'}, use_global_device_ids=true, to_apply=%region_23.0 | all-reduce | flops 1 | bytes 8 | tf_op jit(solution)/shard_map/psum | solution.py:16
  641.3 2.0 fusion.30
  643.3 543.5 %all-reduce.2.cloned.1.call-done = f32[3072,8]{0,1:T(8,128)} async-done(((f32[3072,8]{0,1:T(8,128)}), f32[3072,8]{0,1:T(8,128)}) %all-reduce.2.cloned.1.call-update) | async-done | bytes 98320 | tf_op jit(solution)/shard_map/psum | solution.py:41
  1187.8 3.1 fusion.2
  (49 shorter events, 10.7 us)
Async XLA Ops:
  7.2 122.8 %copy-start = (f32[3072,8]{0,1:T(8,128)S(1)}, f32[3072,8]{0,1:T(8,128)}, u32[]{:S(2)}) copy-start(f32[3072,8]{0,1:T(8,128)} %param.9) | copy-start | bytes 294916
  7.2 3.0 copy-start.1
  7.2 115.1 %all-gather.2.cloned.1.call-start = ((), (), s32[]{:S(2)}) async-start(), calls=%async_computation.1 | async-start | bytes 13369344 | tf_op jit(solution)/shard_map/all_gather | solution.py:30
  10.1 1176.7 %all-reduce.2.cloned.1.call-start = ((), (), s32[]{:S(2)}) async-start(), calls=%async_computation.2 | async-start | bytes 196608 | tf_op jit(solution)/shard_map/psum | solution.py:41
  641.3 549.5 %copy-start.3 = (f32[192,8]{0,1:T(8,128)}, f32[192,8]{0,1:T(8,128)S(1)}, u32[]{:S(2)}) copy-start(f32[192,8]{0,1:T(8,128)S(1)} %stack.41) | copy-start | bytes 18436
  1187.8 3.1 copy-start.2
Sparse Core Ops, SparseCore 0:
  11.7 110.6 all-gather.1
  643.4 543.3 all-reduce.1
where the time goes:
time: 1200 us
  waiting for transfers between devices  636 us (53%)
  blocking collectives  514 us (43%)
  between operations  19.7 us (2%)
  matrix products  16.2 us (1%)
    psum x1, waiting for transfers between devices, on_device(): q_factor = lax.psum(q_local, ('dp', 'fsdp')) / replicas  544 us
    psum x8, blocking collectives, orthonormal_columns(): norm_square = lax.psum(jnp.sum(column * column), 'fsdp')  240 us
    psum x7, blocking collectives, orthonormal_columns(): inner_vals = lax.psum(jnp.dot(column, stacked, precision=highest), 'fsdp')  208 us
    all_gather x1, waiting for transfers between devices, on_device(): lax.all_gather(masked_grad, 'fsdp', axis=0, tiled=True)  92.6 us
    psum x1, blocking collectives, on_device(): p_mean = lax.psum(p_local, 'dp') / replicas  48 us
  transfers between devices with their start and end apart: 2, of which 2 were waited for; matrix products, arithmetic and copies ran while one was open for 0% of the time, Pallas kernels for 0%

commit v1 on v0

--- a/solution.py
+++ b/solution.py
@@ -2,6 +2,7 @@
 import jax.numpy as jnp
 from jax import lax
 from jax.sharding import PartitionSpec as P
+from jax.lax import psum
 
 
 def orthonormal_columns(p_rows):
@@ -38,7 +39,7 @@
     q_local = jnp.einsum(
         "rd,rk->dk", merged, ortho_basis, precision=highest, preferred_element_type=jnp.float32
     )
-    q_factor = lax.psum(q_local, ("dp", "fsdp")) / replicas
+    q_factor = psum(psum(q_local, "dp"), "fsdp") / replicas
     error_next = (merged - jnp.dot(ortho_basis, q_factor.T, precision=highest)).astype(jnp.bfloat16)
     return (ortho_basis, q_factor, error_next[None])
 

time: 1200 us -> 1050 us (0.88)
  waiting for transfers between devices: 636 us -> 492 us
    psum x1 -> x2, waiting for transfers between devices: 544 us -> 400 us  [on_device(): q_factor = psum(psum(q_local, 'dp'), 'fsdp') / replicas]
  transfers between devices with their start and end apart: 2 -> 3, of which waited for: 2 -> 3; matrix products, arithmetic and copies ran while one was open for 0% -> 0% of each run, Pallas kernels for 0% -> 0%
where the time goes in v1:
time: 1050 us
  blocking collectives  514 us (49%)
  waiting for transfers between devices  492 us (47%)
  between operations  19.4 us (2%)
  matrix products  16 us (2%)
  other arithmetic  10.6 us (1%)
    psum x2, waiting for transfers between devices, on_device(): q_factor = psum(psum(q_local, 'dp'), 'fsdp') / replicas  400 us
    psum x8, blocking collectives, orthonormal_columns(): norm_square = lax.psum(jnp.sum(column * column), 'fsdp')  240 us
    psum x7, blocking collectives, orthonormal_columns(): inner_vals = lax.psum(jnp.dot(column, stacked, precision=highest), 'fsdp')  208 us
    all_gather x1, waiting for transfers between devices, on_device(): lax.all_gather(masked_grad, 'fsdp', axis=0, tiled=True)  92.6 us
    psum x1, blocking collectives, on_device(): p_mean = lax.psum(p_local, 'dp') / replicas  48 us
  transfers between devices with their start and end apart: 3, of which 3 were waited for; matrix products, arithmetic and copies ran while one was open for 0% of the time, Pallas kernels for 0%

profile of v1, /device:TPU:1, one launch (start us, length us, event | category | flops | bytes accessed | tf_op | source)
XLA Modules:
  0.0 1053.4 jit_solution(7366049517486373123)
XLA Ops:
  8.0 2.1 broadcast_multiply_fusion
  10.6 19.1 %all_to_all.19 = bf16[128,16,192]{0,2,1:T(8,128)(2,1)S(1)} all-to-all(bf16[128,16,192]{0,2,1:T(8,128)(2,1)S(1)} %bitcast.83), channel_id=1, replica_groups=mesh['dp'=32,'fsdp'=16] {'fsdp'}, dimensions={1} | all-to-all | bytes 1572864 | tf_op jit(solution)/shard_map/all_to_all | solution.py:27
  29.7 92.6 %all-gather.2.cloned.1.call-done = bf16[2048,3072]{1,0:T(8,128)(2,1)} async-done(((bf16[128,3072]{1,0:T(8,128)(2,1)}), bf16[2048,3072]{1,0:T(8,128)(2,1)}) %all-gather.2.cloned.1.call-update) | async-done | bytes 12582928 | tf_op jit(solution)/shard_map/all_gather | solution.py:31
  122.3 7.5 fusion
  131.7 48.0 %psum.126 = f32[192,8]{0,1:T(8,128)S(1)} all-reduce(f32[192,8]{0,1:T(8,128)S(1)} %fusion.29), channel_id=1, replica_groups=mesh['dp'=32,'fsdp'=16] {'dp'}, use_global_device_ids=true, to_apply=%region_0.0 | all-reduce | flops 1536 | bytes 12288 | tf_op jit(solution)/shard_map/psum | solution.py:37
  180.4 31.8 %psum.127 = f32[]{:T(128)} all-reduce(f32[]{:T(128)} %multiply_reduce_fusion.8), channel_id=1, replica_groups=mesh['dp'=32,'fsdp'=16] {'fsdp'}, use_global_device_ids=true, to_apply=%region_2.0 | all-reduce | flops 1 | bytes 8 | tf_op jit(solution)/shard_map/psum | solution.py:17
  213.5 29.1 %psum.128 = f32[]{:T(128)} all-reduce(f32[]{:T(128)} %multiply_reduce_fusion), channel_id=1, replica_groups=mesh['dp'=32,'fsdp'=16] {'fsdp'}, use_global_device_ids=true, to_apply=%region_3.0 | all-reduce | flops 1 | bytes 8 | tf_op jit(solution)/shard_map/psum | solution.py:15
  243.8 30.6 %psum.129 = f32[]{:T(128)} all-reduce(f32[]{:T(128)} %multiply_reduce_fusion.7), channel_id=1, replica_groups=mesh['dp'=32,'fsdp'=16] {'fsdp'}, use_global_device_ids=true, to_apply=%region_5.0 | all-reduce | flops 1 | bytes 8 | tf_op jit(solution)/shard_map/psum | solution.py:17
  275.9 29.1 %psum.130 = f32[2]{0:T(128)S(1)} all-reduce(f32[2]{0:T(128)S(1)} %convolution_bitcast_fusion.6), channel_id=1, replica_groups=mesh['dp'=32,'fsdp'=16] {'fsdp'}, use_global_device_ids=true, to_apply=%region_6.0 | all-reduce | flops 2 | bytes 16 | tf_op jit(solution)/shard_map/psum | solution.py:15
  305.7 30.0 %psum.131 = f32[]{:T(128)} all-reduce(f32[]{:T(128)} %get-tuple-element.13), channel_id=1, replica_groups=mesh['dp'=32,'fsdp'=16] {'fsdp'}, use_global_device_ids=true, to_apply=%region_8.0 | all-reduce | flops 1 | bytes 8 | tf_op jit(solution)/shard_map/psum | solution.py:17
  336.5 29.1 %psum.132 = f32[3]{0:T(128)S(1)} all-reduce(f32[3]{0:T(128)S(1)} %convolution_bitcast_fusion.5), channel_id=1, replica_groups=mesh['dp'=32,'fsdp'=16] {'fsdp'}, use_global_device_ids=true, to_apply=%region_9.0 | all-reduce | flops 3 | bytes 24 | tf_op jit(solution)/shard_map/psum | solution.py:15
  366.4 30.0 %psum.133 = f32[]{:T(128)} all-reduce(f32[]{:T(128)} %get-tuple-element.11), channel_id=1, replica_groups=mesh['dp'=32,'fsdp'=16] {'fsdp'}, use_global_device_ids=true, to_apply=%region_11.0 | all-reduce | flops 1 | bytes 8 | tf_op jit(solution)/shard_map/psum | solution.py:17
  397.2 29.5 %psum.134 = f32[4]{0:T(128)S(1)} all-reduce(f32[4]{0:T(128)S(1)} %convolution_bitcast_fusion.4), channel_id=1, replica_groups=mesh['dp'=32,'fsdp'=16] {'fsdp'}, use_global_device_ids=true, to_apply=%region_12.0 | all-reduce | flops 4 | bytes 32 | tf_op jit(solution)/shard_map/psum | solution.py:15
  427.4 29.6 %psum.135 = f32[]{:T(128)} all-reduce(f32[]{:T(128)} %get-tuple-element.9), channel_id=1, replica_groups=mesh['dp'=32,'fsdp'=16] {'fsdp'}, use_global_device_ids=true, to_apply=%region_14.0 | all-reduce | flops 1 | bytes 8 | tf_op jit(solution)/shard_map/psum | solution.py:17
  457.8 29.8 %psum.136 = f32[5]{0:T(128)S(1)} all-reduce(f32[5]{0:T(128)S(1)} %convolution_bitcast_fusion.3), channel_id=1, replica_groups=mesh['dp'=32,'fsdp'=16] {'fsdp'}, use_global_device_ids=true, to_apply=%region_15.0 | all-reduce | flops 5 | bytes 40 | tf_op jit(solution)/shard_map/psum | solution.py:15
  488.4 29.3 %psum.137 = f32[]{:T(128)} all-reduce(f32[]{:T(128)} %get-tuple-element.7), channel_id=1, replica_groups=mesh['dp'=32,'fsdp'=16] {'fsdp'}, use_global_device_ids=true, to_apply=%region_17.0 | all-reduce | flops 1 | bytes 8 | tf_op jit(solution)/shard_map/psum | solution.py:17
  518.5 30.6 %psum.138 = f32[6]{0:T(128)S(1)} all-reduce(f32[6]{0:T(128)S(1)} %convolution_bitcast_fusion.2), channel_id=1, replica_groups=mesh['dp'=32,'fsdp'=16] {'fsdp'}, use_global_device_ids=true, to_apply=%region_18.0 | all-reduce | flops 6 | bytes 48 | tf_op jit(solution)/shard_map/psum | solution.py:15
  549.9 29.3 %psum.139 = f32[]{:T(128)} all-reduce(f32[]{:T(128)} %get-tuple-element.5), channel_id=1, replica_groups=mesh['dp'=32,'fsdp'=16] {'fsdp'}, use_global_device_ids=true, to_apply=%region_20.0 | all-reduce | flops 1 | bytes 8 | tf_op jit(solution)/shard_map/psum | solution.py:17
  580.0 30.5 %psum.140 = f32[7]{0:T(128)S(1)} all-reduce(f32[7]{0:T(128)S(1)} %convolution_bitcast_fusion.1), channel_id=1, replica_groups=mesh['dp'=32,'fsdp'=16] {'fsdp'}, use_global_device_ids=true, to_apply=%region_21.0 | all-reduce | flops 7 | bytes 56 | tf_op jit(solution)/shard_map/psum | solution.py:15
  611.3 29.1 %psum.141 = f32[]{:T(128)} all-reduce(f32[]{:T(128)} %get-tuple-element.3), channel_id=1, replica_groups=mesh['dp'=32,'fsdp'=16] {'fsdp'}, use_global_device_ids=true, to_apply=%region_23.0 | all-reduce | flops 1 | bytes 8 | tf_op jit(solution)/shard_map/psum | solution.py:17
  641.2 2.0 fusion.30
  643.2 291.4 %all-reduce.3.cloned.1.call-done = f32[3072,8]{0,1:T(8,128)} async-done(((f32[3072,8]{0,1:T(8,128)}), f32[3072,8]{0,1:T(8,128)}) %all-reduce.3.cloned.1.call-update) | async-done | bytes 98320 | tf_op jit(solution)/shard_map/psum | solution.py:42
  934.6 108.2 %all-reduce.5.cloned.1.call-done = f32[3072,8]{0,1:T(8,128)} async-done(((f32[3072,8]{0,1:T(8,128)}), f32[3072,8]{0,1:T(8,128)}) %all-reduce.5.cloned.1.call-update) | async-done | bytes 98320 | tf_op jit(solution)/shard_map/psum | solution.py:42
  1043.8 3.1 fusion.2
  (52 shorter events, 12.6 us)
Async XLA Ops:
  7.2 122.6 %copy-start = (f32[3072,8]{0,1:T(8,128)S(1)}, f32[3072,8]{0,1:T(8,128)}, u32[]{:S(2)}) copy-start(f32[3072,8]{0,1:T(8,128)} %param.9) | copy-start | bytes 294916
  7.2 3.0 copy-start.1
  7.2 115.1 %all-gather.2.cloned.1.call-start = ((), (), s32[]{:S(2)}) async-start(), calls=%async_computation.1 | async-start | bytes 13369344 | tf_op jit(solution)/shard_map/all_gather | solution.py:31
  10.1 924.5 %all-reduce.3.cloned.1.call-start = ((), (), s32[]{:S(2)}) async-start(), calls=%async_computation.2 | async-start | bytes 196608 | tf_op jit(solution)/shard_map/psum | solution.py:42
  641.2 405.7 %copy-start.3 = (f32[192,8]{0,1:T(8,128)}, f32[192,8]{0,1:T(8,128)S(1)}, u32[]{:S(2)}) copy-start(f32[192,8]{0,1:T(8,128)S(1)} %stack.41) | copy-start | bytes 18436
  643.2 399.7 %all-reduce.5.cloned.1.call-start = ((), (), s32[]{:S(2)}) async-start(), calls=%async_computation.3 | async-start | bytes 196608 | tf_op jit(solution)/shard_map/psum | solution.py:42
  1043.8 3.1 copy-start.2
Sparse Core Ops, SparseCore 0:
  11.7 110.6 all-gather.1
  643.3 291.2 all-reduce.2
  938.2 104.6 all-reduce.4
